TPU v7x, 32 devices: a whole 2x2x4 slice. The times are simulated.
32 devices in a mesh: pipe: 4 (over z), blk: 2 (over x), uly: 4 (over y, core).
Axes of the slice: x: 2, y: 2, z: 4, core: 2. Of those that a mesh axis runs over, the one named last changes fastest.
Arguments:
- hidden_in: bfloat16 [4, 64, 3072], P('pipe', ('blk', 'uly')), may hold values from -6 to 6
- text_len: int32 [1], replicated, may hold values from 16 to 64
- qkv_video: bfloat16 [4, 3072, 3, 1536], P('pipe', 'blk', None, 'uly'), may hold values from -0.109375 to 0.109375
- qkv_text: bfloat16 [2, 3072, 3, 1536], P(None, 'blk', None, 'uly'), may hold values from -0.109375 to 0.109375
- out_video: bfloat16 [4, 1536, 3072], P('pipe', 'uly', 'blk'), may hold values from -0.15625 to 0.15625
- out_text: bfloat16 [2, 1536, 3072], P(None, 'uly', 'blk'), may hold values from -0.15625 to 0.15625
- modulation: float32 [4, 2, 3, 3072], P('pipe'), may hold values from -3 to 3
- qk_gain: float32 [4, 2, 2, 128], P('pipe'), may hold values from 1 to 3
- stale_kv: bfloat16 [4, 2, 256, 1536], P('pipe', None, None, 'uly'), may hold values from -24 to 24, as said below
Outputs:
- hidden_out: bfloat16 [4, 64, 3072], P('pipe', ('blk', 'uly'))
Inputs may be any that keep to these rules, and one draw needn't show every extreme that they name: `stale_kv`: stale keys and values of order one, some keys larger.
All inputs are finite; a program needn't handle non-finite values.
Results may differ from a plain program's by a relative error of at most 0.04.
Values may be sent and summed in bfloat16 or wider, within the bound.
A program may use at most 128 MiB of HBM per device.

v0:
```python
import math

import jax
import jax.numpy as jnp
from jax import lax
from jax.sharding import PartitionSpec as P


def from_behind(shard, axis, by):
    size = lax.axis_size(axis)
    pairs = [(i, i + by) for i in range(size) if 0 <= i + by < size]
    return lax.ppermute(shard, axis, pairs)


def rms_scale(values, gain):
    squares = jnp.mean(values * values, axis=-1, keepdims=True)
    return values * lax.rsqrt(squares + 1e-06) * gain


def local(
    hidden_in, text_len, qkv_video, qkv_text, out_video, out_text, modulation, qk_gain, stale_kv
):
    sections = lax.axis_size("pipe")
    blk_count = lax.axis_size("blk")
    uly_count = lax.axis_size("uly")
    section = lax.axis_index("pipe")
    blk_index = lax.axis_index("blk")
    rows = hidden_in.shape[1]
    width = hidden_in.shape[2]
    group = rows * uly_count
    micro = group * blk_count
    text_count = 2 * group
    dual_count = qkv_text.shape[0]
    head_dim = qk_gain.shape[3]
    local_width = stale_kv.shape[3]
    local_heads = local_width // head_dim
    inv_scale = 1.0 / math.sqrt(head_dim)
    dual = section < dual_count
    chosen = jnp.minimum(section, dual_count - 1)
    text_rows_w = lax.dynamic_index_in_dim(qkv_text, chosen, 0, keepdims=False)
    text_cols_w = lax.dynamic_index_in_dim(out_text, chosen, 0, keepdims=False)
    video_proj, text_proj, video_back, text_back = (
        lax.all_gather(qkv_video[0], "blk", axis=0, tiled=True),
        lax.all_gather(text_rows_w, "blk", axis=0, tiled=True),
        lax.all_gather(out_video[0], "blk", axis=1, tiled=True),
        lax.all_gather(text_cols_w, "blk", axis=1, tiled=True),
    )
    video_proj = video_proj.reshape(width, 3 * local_width)
    text_proj = text_proj.reshape(width, 3 * local_width)
    mods = modulation[0]
    gains = qk_gain[0]
    stale = stale_kv[0]
    valid_text = text_len[0]
    cache_keys = stale[0]
    cache_values = stale[1]
    places = jnp.arange(micro * sections, dtype=jnp.int32)
    key_ok = (places >= text_count) | (places < valid_text)
    carried = jnp.zeros((rows, width), jnp.bfloat16)
    inbox = hidden_in[0]
    outbox = jnp.zeros((rows, width), jnp.bfloat16)
    last_tick = 2 * sections - 2
    for tick in range(2 * sections - 1):
        micro_index = tick - section
        valid = (micro_index >= 0) & (micro_index < sections)
        current = jnp.clip(micro_index, 0, sections - 1)
        entering = jnp.where(section == 0, inbox, carried)
        is_text = dual & (current * micro + blk_index * group < text_count)
        stream = is_text.astype(jnp.int32)
        mod_rows = lax.dynamic_index_in_dim(mods, stream, 0, keepdims=False)
        gain_rows = lax.dynamic_index_in_dim(gains, stream, 0, keepdims=False)
        floats = entering.astype(jnp.float32)
        centred = floats - jnp.mean(floats, axis=-1, keepdims=True)
        normed = centred * lax.rsqrt(jnp.mean(centred * centred, axis=-1, keepdims=True) + 1e-06)
        modded = (normed * (1.0 + mod_rows[1]) + mod_rows[0]).astype(jnp.bfloat16)
        gathered = lax.all_gather(modded, "uly", axis=0, tiled=True)
        projected = lax.cond(
            is_text,
            lambda operand: jnp.dot(operand, text_proj, preferred_element_type=jnp.float32),
            lambda operand: jnp.dot(operand, video_proj, preferred_element_type=jnp.float32),
            gathered,
        )
        projected = projected.reshape(group, 3, local_heads, head_dim)
        queries = rms_scale(projected[:, 0], gain_rows[0]).astype(jnp.bfloat16)
        fresh_keys = (
            rms_scale(projected[:, 1], gain_rows[1])
            .astype(jnp.bfloat16)
            .reshape(group, local_width)
        )
        fresh_values = projected[:, 2].astype(jnp.bfloat16).reshape(group, local_width)
        all_keys, all_values = (
            lax.all_gather(fresh_keys, "blk", axis=0, tiled=True),
            lax.all_gather(fresh_values, "blk", axis=0, tiled=True),
        )
        offset = current * micro
        old_keys = lax.dynamic_slice_in_dim(cache_keys, offset, micro, 0)
        old_values = lax.dynamic_slice_in_dim(cache_values, offset, micro, 0)
        cache_keys = lax.dynamic_update_slice_in_dim(
            cache_keys, jnp.where(valid, all_keys, old_keys), offset, 0
        )
        cache_values = lax.dynamic_update_slice_in_dim(
            cache_values, jnp.where(valid, all_values, old_values), offset, 0
        )
        key_heads = cache_keys.reshape(-1, local_heads, head_dim)
        value_heads = cache_values.reshape(-1, local_heads, head_dim)
        scores = (
            jnp.einsum("rhd,lhd->hrl", queries, key_heads, preferred_element_type=jnp.float32)
            * inv_scale
        )
        scores = jnp.where(key_ok[None, None, :], scores, -1e30)
        peak = jnp.max(scores, axis=-1, keepdims=True)
        weights = jnp.where(key_ok[None, None, :], jnp.exp(scores - peak), 0.0)
        total = jnp.sum(weights, axis=-1)
        mixed = jnp.einsum(
            "hrl,lhd->rhd",
            weights.astype(jnp.bfloat16),
            value_heads,
            preferred_element_type=jnp.float32,
        )
        attended = (
            (mixed / jnp.transpose(total)[:, :, None])
            .reshape(group, local_width)
            .astype(jnp.bfloat16)
        )
        partial_value = lax.cond(
            is_text,
            lambda operand: jnp.dot(operand, text_back, preferred_element_type=jnp.float32),
            lambda operand: jnp.dot(operand, video_back, preferred_element_type=jnp.float32),
            attended,
        )
        summed = lax.psum_scatter(partial_value, "uly", scatter_dimension=0, tiled=True)
        leaving = (floats + mod_rows[2] * summed).astype(jnp.bfloat16)
        outbox = jnp.where((section == sections - 1) & valid, leaving, outbox)
        if tick < last_tick:
            carried = from_behind(leaving, "pipe", 1)
            inbox, outbox = from_behind((inbox, outbox), "pipe", -1)
    return outbox[None]


def solution(mesh):
    return jax.shard_map(
        local,
        mesh=mesh,
        in_specs=(
            P("pipe", ("blk", "uly"), None),
            P(),
            P("pipe", "blk", None, "uly"),
            P(None, "blk", None, "uly"),
            P("pipe", "uly", "blk"),
            P(None, "uly", "blk"),
            P("pipe", None, None, None),
            P("pipe", None, None, None),
            P("pipe", None, None, "uly"),
        ),
        out_specs=P("pipe", ("blk", "uly"), None),
        check_vma=False,
    )
```

profile of v0, /device:TPU:25, one launch (start us, length us, event | category | flops | bytes accessed | tf_op | source)
XLA Modules:
  0.0 630.1 jit_solution(11148494798743195502)
XLA Ops:
  6.5 4.2 constant_dynamic-slice_fusion.23
  10.8 6.1 copy.199
  16.9 6.1 copy.109
  30.0 6.1 all_gather.75
  36.1 71.1 %all-gather.11.cloned.1.call-done = bf16[1,3072,3,384]{1,3,2,0:T(8,128)(2,1)} async-done(((bf16[1,1536,3,384]{1,3,2,0:T(8,128)(2,1)}), bf16[1,3072,3,384]{1,3,2,0:T(8,128)(2,1)}) %all-gather.11.cloned.1.call-update) | async-done | bytes 7077904 | tf_op jit(solution)/shard_map/all_gather | solution.py:44
  107.3 90.8 %all-gather.9.cloned.1.call-done = bf16[1,3072,3,384]{1,3,2,0:T(8,128)(2,1)} async-done(((bf16[1,1536,3,384]{1,3,2,0:T(8,128)(2,1)}), bf16[1,3072,3,384]{1,3,2,0:T(8,128)(2,1)}) %all-gather.9.cloned.1.call-update) | async-done | bytes 7077904 | tf_op jit(solution)/shard_map/all_gather | solution.py:43
  198.1 5.2 conditional.14
  198.1 5.2 fusion.170
  203.6 3.4 all_gather.79
  207.0 3.5 all_gather.78
  212.4 23.9 %all-gather.15.cloned.1.call-done = bf16[1,384,3072]{2,1,0:T(8,128)(2,1)} async-done(((bf16[1,384,1536]{2,1,0:T(8,128)(2,1)}), bf16[1,384,3072]{2,1,0:T(8,128)(2,1)}) %all-gather.15.cloned.1.call-update) | async-done | bytes 2359312 | tf_op jit(solution)/shard_map/all_gather | solution.py:46
  236.2 37.4 %all-gather.13.cloned.1.call-done = bf16[1,384,3072]{2,1,0:T(8,128)(2,1)} async-done(((bf16[1,384,1536]{2,1,0:T(8,128)(2,1)}), bf16[1,384,3072]{2,1,0:T(8,128)(2,1)}) %all-gather.13.cloned.1.call-update) | async-done | bytes 2359312 | tf_op jit(solution)/shard_map/all_gather | solution.py:45
  278.8 18.7 %reduce-scatter.8.cloned.1.call-done = f32[8,3072]{1,0:T(8,128)} async-done(((f32[32,3072]{1,0:T(8,128)}), f32[8,3072]{1,0:T(8,128)}) %reduce-scatter.8.cloned.1.call-update) | async-done | bytes 98320 | tf_op jit(solution)/shard_map/reduce_scatter | solution.py:130
  299.8 3.5 collective-permute-done.6
  303.8 7.3 %all_gather.82 = bf16[32,3072]{1,0:T(8,128)(2,1)S(1)} all-gather(bf16[8,3072]{1,0:T(8,128)(2,1)S(1)} %fusion.93), channel_id=1, replica_groups=mesh['pipe'=4,'blk'=2,'uly'=4] {'uly'}, dimensions={0}, use_global_device_ids=true | all-gather | bytes 245760 | tf_op jit(solution)/shard_map/all_gather | solution.py:75
  311.1 5.2 conditional.16
  311.1 5.2 fusion.174
  316.7 3.5 all_gather.84
  320.9 3.4 all_gather.83
  325.6 2.2 conditional.17
  333.5 17.8 %reduce-scatter.10.cloned.1.call-done = f32[8,3072]{1,0:T(8,128)} async-done(((f32[32,3072]{1,0:T(8,128)}), f32[8,3072]{1,0:T(8,128)}) %reduce-scatter.10.cloned.1.call-update) | async-done | bytes 98320 | tf_op jit(solution)/shard_map/reduce_scatter | solution.py:130
  353.6 3.5 collective-permute-done.7
  358.3 7.3 %all_gather.85 = bf16[32,3072]{1,0:T(8,128)(2,1)S(1)} all-gather(bf16[8,3072]{1,0:T(8,128)(2,1)S(1)} %fusion.89), channel_id=1, replica_groups=mesh['pipe'=4,'blk'=2,'uly'=4] {'uly'}, dimensions={0}, use_global_device_ids=true | all-gather | bytes 245760 | tf_op jit(solution)/shard_map/all_gather | solution.py:75
  365.6 5.2 conditional.18
  365.6 5.2 fusion.178
  371.2 3.4 all_gather.87
  375.2 3.4 all_gather.86
  379.9 2.2 conditional.19
  385.7 2.9 collective-permute-start.2
  388.5 17.1 %reduce-scatter.12.cloned.1.call-done = f32[8,3072]{1,0:T(8,128)} async-done(((f32[32,3072]{1,0:T(8,128)}), f32[8,3072]{1,0:T(8,128)}) %reduce-scatter.12.cloned.1.call-update) | async-done | bytes 98320 | tf_op jit(solution)/shard_map/reduce_scatter | solution.py:130
  407.9 3.5 collective-permute-done.8
  411.9 7.3 %all_gather.88 = bf16[32,3072]{1,0:T(8,128)(2,1)S(1)} all-gather(bf16[8,3072]{1,0:T(8,128)(2,1)S(1)} %fusion.85), channel_id=1, replica_groups=mesh['pipe'=4,'blk'=2,'uly'=4] {'uly'}, dimensions={0}, use_global_device_ids=true | all-gather | bytes 245760 | tf_op jit(solution)/shard_map/all_gather | solution.py:75
  419.2 5.2 conditional.20
  419.2 5.2 fusion.182
  424.9 3.6 all_gather.90
  429.1 3.4 all_gather.89
  433.8 2.2 conditional.21
  436.8 2.9 collective-permute-start.14
  441.6 17.8 %reduce-scatter.14.cloned.1.call-done = f32[8,3072]{1,0:T(8,128)} async-done(((f32[32,3072]{1,0:T(8,128)}), f32[8,3072]{1,0:T(8,128)}) %reduce-scatter.14.cloned.1.call-update) | async-done | bytes 98320 | tf_op jit(solution)/shard_map/reduce_scatter | solution.py:130
  461.7 3.5 collective-permute-done.9
  465.7 7.3 %all_gather.91 = bf16[32,3072]{1,0:T(8,128)(2,1)S(1)} all-gather(bf16[8,3072]{1,0:T(8,128)(2,1)S(1)} %fusion.81), channel_id=1, replica_groups=mesh['pipe'=4,'blk'=2,'uly'=4] {'uly'}, dimensions={0}, use_global_device_ids=true | all-gather | bytes 245760 | tf_op jit(solution)/shard_map/all_gather | solution.py:75
  473.0 5.2 conditional.22
  473.0 5.2 fusion.186
  478.6 3.4 all_gather.93
  483.0 3.4 all_gather.92
  492.4 2.9 collective-permute-start.4
  495.3 18.5 %reduce-scatter.16.cloned.1.call-done = f32[8,3072]{1,0:T(8,128)} async-done(((f32[32,3072]{1,0:T(8,128)}), f32[8,3072]{1,0:T(8,128)}) %reduce-scatter.16.cloned.1.call-update) | async-done | bytes 98320 | tf_op jit(solution)/shard_map/reduce_scatter | solution.py:130
  516.0 3.5 collective-permute-done.10
  520.0 7.3 %all_gather.94 = bf16[32,3072]{1,0:T(8,128)(2,1)S(1)} all-gather(bf16[8,3072]{1,0:T(8,128)(2,1)S(1)} %fusion.77), channel_id=1, replica_groups=mesh['pipe'=4,'blk'=2,'uly'=4] {'uly'}, dimensions={0}, use_global_device_ids=true | all-gather | bytes 245760 | tf_op jit(solution)/shard_map/all_gather | solution.py:75
  527.3 5.2 conditional.24
  527.3 5.2 fusion.190
  532.9 3.6 all_gather.96
  537.1 3.4 all_gather.95
  541.7 2.2 conditional.25
  544.7 2.9 collective-permute-start.16
  549.8 17.6 %reduce-scatter.18.cloned.1.call-done = f32[8,3072]{1,0:T(8,128)} async-done(((f32[32,3072]{1,0:T(8,128)}), f32[8,3072]{1,0:T(8,128)}) %reduce-scatter.18.cloned.1.call-update) | async-done | bytes 98320 | tf_op jit(solution)/shard_map/reduce_scatter | solution.py:130
  569.7 3.5 collective-permute-done.11
  573.7 7.3 %all_gather.97 = bf16[32,3072]{1,0:T(8,128)(2,1)S(1)} all-gather(bf16[8,3072]{1,0:T(8,128)(2,1)S(1)} %fusion.73), channel_id=1, replica_groups=mesh['pipe'=4,'blk'=2,'uly'=4] {'uly'}, dimensions={0}, use_global_device_ids=true | all-gather | bytes 245760 | tf_op jit(solution)/shard_map/all_gather | solution.py:75
  581.0 5.2 conditional.26
  581.0 5.2 fusion.194
  586.6 3.4 all_gather.99
  590.9 3.4 all_gather.98
  595.9 2.2 conditional.27
  602.2 19.4 %reduce-scatter.20.cloned.1.call-done = f32[8,3072]{1,0:T(8,128)} async-done(((f32[32,3072]{1,0:T(8,128)}), f32[8,3072]{1,0:T(8,128)}) %reduce-scatter.20.cloned.1.call-update) | async-done | bytes 98320 | tf_op jit(solution)/shard_map/reduce_scatter | solution.py:130
  (302 shorter events, 85.5 us)
Async XLA Ops:
  6.5 16.6 %copy-start = (bf16[2,384,1536]{2,1,0:T(8,128)(2,1)S(1)}, bf16[2,384,1536]{2,1,0:T(8,128)(2,1)}, u32[]{:S(2)}) copy-start(bf16[2,384,1536]{2,1,0:T(8,128)(2,1)} %param.42) | copy-start | bytes 7077892
  6.5 100.7 %all-gather.11.cloned.1.call-start = ((), (), s32[]{:S(2)}) async-start(), calls=%async_computation.15 | async-start | bytes 10616832 | tf_op jit(solution)/shard_map/all_gather | solution.py:44
  16.9 181.2 %all-gather.9.cloned.1.call-start = ((), (), s32[]{:S(2)}) async-start(), calls=%async_computation.14 | async-start | bytes 10616832 | tf_op jit(solution)/shard_map/all_gather | solution.py:43
  23.0 1.9 copy-start.9
  23.1 5.4 copy-start.11
  23.1 6.0 copy-start.8
  23.1 213.2 %all-gather.15.cloned.1.call-start = ((), (), s32[]{:S(2)}) async-start(), calls=%async_computation.17 | async-start | bytes 3538944 | tf_op jit(solution)/shard_map/all_gather | solution.py:46
  24.3 249.4 %all-gather.13.cloned.1.call-start = ((), (), s32[]{:S(2)}) async-start(), calls=%async_computation.16 | async-start | bytes 3538944 | tf_op jit(solution)/shard_map/all_gather | solution.py:45
  24.9 272.7 %reduce-scatter.8.cloned.1.call-start = ((), (), s32[]{:S(2)}) async-start(), calls=%async_computation.7 | async-start | bytes 491520 | tf_op jit(solution)/shard_map/reduce_scatter | solution.py:130
  198.1 13.7 %copy-start.19 = (pred[256]{0:T(512)(128)(4,1)S(1)}, pred[256]{0:T(512)(128)(4,1)}, u32[]{:S(2)}) copy-start(pred[256]{0:T(512)(128)(4,1)} %compare_or_fusion) | copy-start | bytes 772
  211.6 67.3 %copy-start.16 = (f32[1,1,2,128]{3,2,1,0:T(2,128)S(1)}, f32[1,1,2,128]{3,2,1,0:T(2,128)}, u32[]{:S(2)}) copy-start(f32[1,1,2,128]{3,2,1,0:T(2,128)} %get-tuple-element.336) | copy-start | bytes 3076
  275.8 0.8 copy-start.1
  276.6 74.7 %reduce-scatter.10.cloned.1.call-start = ((), (), s32[]{:S(2)}) async-start(), calls=%async_computation.8 | async-start | bytes 491520 | tf_op jit(solution)/shard_map/reduce_scatter | solution.py:130
  276.6 23.2 %collective-permute-start = (bf16[8,3072]{1,0:T(8,128)(2,1)S(1)}, bf16[8,3072]{1,0:T(8,128)(2,1)S(1)}, u32[]{:S(2)}, u32[]{:S(2)}) collective-permute-start(bf16[8,3072]{1,0:T(8,128)(2,1)S(1)} %bitcast.470), channel_id=1, source_target_pairs={{8,0},{16,8},{24,16},{9,1},{17,9},{25,17},{10,2},{18,10},{26,18},{... | collective-permute-start | bytes 147464 | tf_op jit(solution)/shard_map/ppermute | solution.py:12
  298.5 4.8 collective-permute-start.6
  311.1 14.0 %copy-start.20 = (pred[256]{0:T(512)(128)(4,1)S(1)}, pred[256]{0:T(512)(128)(4,1)}, u32[]{:S(2)}) copy-start(pred[256]{0:T(512)(128)(4,1)} %compare_or_fusion) | copy-start | bytes 772
  324.5 6.3 copy-start.15
  327.8 0.8 copy-start.2
  328.6 77.1 %reduce-scatter.12.cloned.1.call-start = ((), (), s32[]{:S(2)}) async-start(), calls=%async_computation.9 | async-start | bytes 491520 | tf_op jit(solution)/shard_map/reduce_scatter | solution.py:130
  328.6 4.9 collective-permute-start.12
  331.3 22.3 %collective-permute-start.1 = (bf16[8,3072]{1,0:T(8,128)(2,1)S(1)}, bf16[8,3072]{1,0:T(8,128)(2,1)S(1)}, u32[]{:S(2)}, u32[]{:S(2)}) collective-permute-start(bf16[8,3072]{1,0:T(8,128)(2,1)S(1)} %collective-permute-done), channel_id=1, source_target_pairs={{8,0},{16,8},{24,16},{9,1},{17,9},{25,17},{10,2},{18,10},{26,18},{... | collective-permute-start | bytes 147464 | tf_op jit(solution)/shard_map/ppermute | solution.py:12
  352.3 4.8 collective-permute-start.7
  365.6 13.7 %copy-start.17 = (f32[128]{0:T(128)S(1)}, f32[128]{0:T(128)}, u32[]{:S(2)}) copy-start(f32[128]{0:T(128)} %get-tuple-element.347) | copy-start | bytes 1540
  365.6 13.8 %copy-start.21 = (pred[256]{0:T(512)(128)(4,1)S(1)}, pred[256]{0:T(512)(128)(4,1)}, u32[]{:S(2)}) copy-start(pred[256]{0:T(512)(128)(4,1)} %compare_or_fusion) | copy-start | bytes 772
  378.8 6.3 copy-start.14
  379.7 32.1 %copy-start.10 = (f32[1,1,1,3072]{3,1,2,0:T(1,128)S(1)}, f32[1,1,1,3072]{3,1,2,0:T(1,128)}, u32[]{:S(2)}) copy-start(f32[1,1,1,3072]{3,1,2,0:T(1,128)} %get-tuple-element.326) | copy-start | bytes 36868
  382.1 0.8 copy-start.3
  382.9 76.6 %reduce-scatter.14.cloned.1.call-start = ((), (), s32[]{:S(2)}) async-start(), calls=%async_computation.10 | async-start | bytes 491520 | tf_op jit(solution)/shard_map/reduce_scatter | solution.py:130
  383.0 5.6 collective-permute-start.13
  385.7 22.2 %collective-permute-start.2 = (bf16[8,3072]{1,0:T(8,128)(2,1)S(1)}, bf16[8,3072]{1,0:T(8,128)(2,1)S(1)}, u32[]{:S(2)}, u32[]{:S(2)}) collective-permute-start(bf16[8,3072]{1,0:T(8,128)(2,1)S(1)} %collective-permute-done.1), channel_id=1, source_target_pairs={{8,0},{16,8},{24,16},{9,1},{17,9},{25,17},{10,2},{18,10},{26,18},{... | collective-permute-start | bytes 147464 | tf_op jit(solution)/shard_map/ppermute | solution.py:12
  406.6 4.8 collective-permute-start.8
  419.2 13.9 %copy-start.18 = (f32[128]{0:T(128)S(1)}, f32[128]{0:T(128)}, u32[]{:S(2)}) copy-start(f32[128]{0:T(128)} %get-tuple-element.345) | copy-start | bytes 1540
  419.2 14.1 %copy-start.22 = (pred[256]{0:T(512)(128)(4,1)S(1)}, pred[256]{0:T(512)(128)(4,1)}, u32[]{:S(2)}) copy-start(pred[256]{0:T(512)(128)(4,1)} %compare_or_fusion) | copy-start | bytes 772
  432.7 7.0 %copy-start.13 = (f32[1,1,2,128]{3,2,1,0:T(2,128)S(1)}, f32[1,1,2,128]{3,2,1,0:T(2,128)}, u32[]{:S(2)}) copy-start(f32[1,1,2,128]{3,2,1,0:T(2,128)} %get-tuple-element.333) | copy-start | bytes 3076
  436.0 0.8 copy-start.4
  436.8 77.0 %reduce-scatter.16.cloned.1.call-start = ((), (), s32[]{:S(2)}) async-start(), calls=%async_computation.11 | async-start | bytes 491520 | tf_op jit(solution)/shard_map/reduce_scatter | solution.py:130
  436.8 4.8 collective-permute-start.14
  439.7 22.0 %collective-permute-start.3 = (bf16[8,3072]{1,0:T(8,128)(2,1)S(1)}, bf16[8,3072]{1,0:T(8,128)(2,1)S(1)}, u32[]{:S(2)}, u32[]{:S(2)}) collective-permute-start(bf16[8,3072]{1,0:T(8,128)(2,1)S(1)} %collective-permute-done.2), channel_id=1, source_target_pairs={{8,0},{16,8},{24,16},{9,1},{17,9},{25,17},{10,2},{18,10},{26,18},{... | collective-permute-start | bytes 147464 | tf_op jit(solution)/shard_map/ppermute | solution.py:12
  460.4 4.8 collective-permute-start.9
  486.6 5.8 copy-start.12
  490.2 0.8 copy-start.5
  491.0 76.4 %reduce-scatter.18.cloned.1.call-start = ((), (), s32[]{:S(2)}) async-start(), calls=%async_computation.12 | async-start | bytes 491520 | tf_op jit(solution)/shard_map/reduce_scatter | solution.py:130
  491.1 4.2 collective-permute-start.15
  492.4 23.6 %collective-permute-start.4 = (bf16[8,3072]{1,0:T(8,128)(2,1)S(1)}, bf16[8,3072]{1,0:T(8,128)(2,1)S(1)}, u32[]{:S(2)}, u32[]{:S(2)}) collective-permute-start(bf16[8,3072]{1,0:T(8,128)(2,1)S(1)} %collective-permute-done.3), channel_id=1, source_target_pairs={{8,0},{16,8},{24,16},{9,1},{17,9},{25,17},{10,2},{18,10},{26,18},{... | collective-permute-start | bytes 147464 | tf_op jit(solution)/shard_map/ppermute | solution.py:12
  514.7 4.8 collective-permute-start.10
  543.9 0.8 copy-start.6
  544.7 76.9 %reduce-scatter.20.cloned.1.call-start = ((), (), s32[]{:S(2)}) async-start(), calls=%async_computation.13 | async-start | bytes 491520 | tf_op jit(solution)/shard_map/reduce_scatter | solution.py:130
  544.7 5.0 collective-permute-start.16
  547.6 22.1 %collective-permute-start.5 = (bf16[8,3072]{1,0:T(8,128)(2,1)S(1)}, bf16[8,3072]{1,0:T(8,128)(2,1)S(1)}, u32[]{:S(2)}, u32[]{:S(2)}) collective-permute-start(bf16[8,3072]{1,0:T(8,128)(2,1)S(1)} %collective-permute-done.4), channel_id=1, source_target_pairs={{8,0},{16,8},{24,16},{9,1},{17,9},{25,17},{10,2},{18,10},{26,18},{... | collective-permute-start | bytes 147464 | tf_op jit(solution)/shard_map/ppermute | solution.py:12
  568.4 4.8 collective-permute-start.11
  598.1 0.8 copy-start.7
  598.8 3.3 collective-permute-start.17
Sparse Core Ops, SparseCore 0:
  17.0 90.2 all-gather.10
  108.8 89.2 all-gather.8
  199.6 36.5 all-gather.14
  237.6 35.9 all-gather.12
  276.7 20.7 reduce-scatter.7
  328.7 22.5 reduce-scatter.9
  383.0 22.5 reduce-scatter.11
  436.9 22.5 reduce-scatter.13
  491.1 22.5 reduce-scatter.15
  544.8 22.5 reduce-scatter.17
  599.0 22.5 reduce-scatter.19
where the time goes:
time: 641 us; the launch traced here: 630 us
  waiting for transfers between devices  373 us (58%)
  blocking collectives  97.6 us (15%)
  matrix products  55.1 us (9%)
  local copies, waits for them, and re-layouts  36.4 us (6%)
  starting transfers between devices  35.8 us (6%)
  between operations  16 us (2%)
  other arithmetic  15.9 us (2%)
    reduce_scatter x7, waiting for transfers between devices, local(): lax.psum_scatter(partial_value, 'uly', scatter_dimension=0, tiled=True)  127 us
    all_gather x1, waiting for transfers between devices, local(): lax.all_gather(qkv_video[0], 'blk', axis=0, tiled=True)  90.8 us
    all_gather x1, waiting for transfers between devices, local(): lax.all_gather(text_rows_w, 'blk', axis=0, tiled=True)  71.1 us
    all_gather x7, blocking collectives, local(): gathered = lax.all_gather(modded, 'uly', axis=0, tiled=True)  49.9 us
    all_gather x1, waiting for transfers between devices, local(): lax.all_gather(out_video[0], 'blk', axis=1, tiled=True)  37.4 us
    dot_general x7, matrix products, local(): jnp.dot(operand, video_proj, preferred_element_type=jnp.float32)  36.2 us
    ppermute x18, starting transfers between devices, from_behind(): return lax.ppermute(shard, axis, pairs)  35.4 us
    all_gather x7, blocking collectives, local(): lax.all_gather(fresh_keys, 'blk', axis=0, tiled=True)  24.1 us
  transfers between devices with their start and end apart: 29, of which 18 were waited for; matrix products, arithmetic and copies ran while one was open for 4% of the time, Pallas kernels for 0%

commit v1 on v0

--- a/solution.py
+++ b/solution.py
@@ -1,9 +1,383 @@
+import functools
 import math
 
 import jax
 import jax.numpy as jnp
 from jax import lax
+from jax.experimental import pallas as pl
+from jax.experimental.pallas import tpu as pltpu
 from jax.sharding import PartitionSpec as P
+
+MESH = pl.DeviceIdType.MESH
+
+
+def unslab(value):
+    count, _, half = value.shape
+    joined = jnp.concatenate([value[:, :8], value[:, 8:]], axis=2)
+    return joined.reshape(count * 8, 2 * half)
+
+
+def slab(value):
+    rows, width = value.shape
+    split = value.reshape(rows // 8, 8, width)
+    return jnp.concatenate([split[:, :, : width // 2], split[:, :, width // 2 :]], axis=1)
+
+
+def pipe_kernel(
+    sections, dual_count, heads, head_dim,
+    bias_ref, hin_ref, mods_ref, gains_ref, wqv_ref, wqt_ref, wov_ref, wot_ref, stale_ref,
+    out_ref,
+    hid, hnew, obuf, stat_out, stat_in, part_own, part_out, part_in, y_own, y_out, y_in,
+    wq, wo, kv,
+    init_sem, hid_sem, stat_ssem, stat_rsem, part_ssem, part_rsem, y_ssem, y_rsem,
+    next_sem, out_sem, wq_sem, wo_sem, kv_sem,
+):
+    s = lax.axis_index("pipe")
+    i = lax.axis_index("blk")
+    j = lax.axis_index("uly")
+    me = (s * 2 + i) * 4 + j
+    local_width = heads * head_dim
+    half = mods_ref.shape[2]
+    micro = 64
+    inv_scale = 1.0 / math.sqrt(head_dim)
+    last = sections - 1
+
+    for c in range(3):
+        @pl.when(s < dual_count)
+        def _():
+            pltpu.make_async_copy(wqt_ref.at[c], wq.at[0, c], wq_sem.at[0, c]).start()
+
+        @pl.when(s >= dual_count)
+        def _():
+            pltpu.make_async_copy(wqv_ref.at[c], wq.at[0, c], wq_sem.at[0, c]).start()
+
+    @pl.when(s < dual_count)
+    def _():
+        pltpu.make_async_copy(wot_ref, wo.at[0], wo_sem.at[0]).start()
+
+    @pl.when(s >= dual_count)
+    def _():
+        pltpu.make_async_copy(wov_ref, wo.at[0], wo_sem.at[0]).start()
+
+    pltpu.make_async_copy(stale_ref, kv, kv_sem.at[0]).start()
+    for c in range(3):
+        pltpu.make_async_copy(wqv_ref.at[c], wq.at[1, c], wq_sem.at[1, c]).start()
+    pltpu.make_async_copy(wov_ref, wo.at[1], wo_sem.at[1]).start()
+
+    barrier = pltpu.get_barrier_semaphore()
+    devices = sections * 8
+
+    @pl.loop(0, devices)
+    def _(d):
+        @pl.when(d != me)
+        def _():
+            pl.semaphore_signal(
+                barrier, inc=1, device_id=(d // 8, (d // 4) % 2, d % 4), device_id_type=MESH
+            )
+
+    pl.semaphore_wait(barrier, devices - 1)
+
+    def init_copy(k):
+        return pltpu.make_async_remote_copy(
+            src_ref=hin_ref.at[k // 4],
+            dst_ref=hid.at[s, i * 4 + j],
+            send_sem=init_sem.at[k],
+            recv_sem=hid_sem.at[s, i * 4 + j],
+            device_id=(0, k // 4, k % 4),
+            device_id_type=MESH,
+        )
+
+    for k in range(8):
+        @pl.when(me != k)
+        def _():
+            init_copy(k).start()
+
+        @pl.when(me == k)
+        def _():
+            pltpu.make_async_copy(
+                hin_ref.at[k // 4], hid.at[s, i * 4 + j], hid_sem.at[s, i * 4 + j]
+            ).start()
+
+    def stat_copy(m):
+        return pltpu.make_async_remote_copy(
+            src_ref=stat_out.at[m], dst_ref=stat_in.at[m],
+            send_sem=stat_ssem.at[m], recv_sem=stat_rsem.at[m],
+            device_id=(s, 1 - i, j), device_id_type=MESH,
+        )
+
+    def part_copy(m, c):
+        return pltpu.make_async_remote_copy(
+            src_ref=part_out.at[m, c], dst_ref=part_in.at[m, c],
+            send_sem=part_ssem.at[m, c], recv_sem=part_rsem.at[m, c],
+            device_id=(s, 1 - i, j), device_id_type=MESH,
+        )
+
+    def y_copy(m, o):
+        to = (j + o) % 4
+        return pltpu.make_async_remote_copy(
+            src_ref=y_out.at[m, to], dst_ref=y_in.at[m, o - 1],
+            send_sem=y_ssem.at[m, o - 1], recv_sem=y_rsem.at[m, o - 1],
+            device_id=(s, i, to), device_id_type=MESH,
+        )
+
+    def next_copy(m, to):
+        return pltpu.make_async_remote_copy(
+            src_ref=hnew.at[m], dst_ref=hid.at[m, pl.ds(2 * j, 2)],
+            send_sem=next_sem.at[m, to], recv_sem=hid_sem.at[m, j],
+            device_id=(s + 1, i, to), device_id_type=MESH,
+        )
+
+    def out_copy(m, e):
+        g = 2 * j + e
+        return pltpu.make_async_remote_copy(
+            src_ref=hnew.at[m, e], dst_ref=obuf.at[i],
+            send_sem=next_sem.at[m, e], recv_sem=out_sem.at[i],
+            device_id=(m, g // 4, g % 4), device_id_type=MESH,
+        )
+
+    def owner(m, e):
+        return m * 8 + 2 * j + e
+
+    def stage_a(m):
+        @pl.when(s == 0)
+        def _():
+            for r in range(8):
+                pltpu.make_async_copy(hid.at[m, r], hid.at[m, r], hid_sem.at[m, r]).wait()
+
+        @pl.when(s > 0)
+        def _():
+            for r in range(4):
+                pair = hid.at[m, pl.ds(2 * r, 2)]
+                pltpu.make_async_copy(pair, pair, hid_sem.at[m, r]).wait()
+
+        floats = unslab(hid[m].astype(jnp.float32))
+        mean = jnp.mean(floats, axis=-1, keepdims=True)
+        centred = floats - mean
+        spread = jnp.sum(centred * centred, axis=-1, keepdims=True)
+        lanes = lax.broadcasted_iota(jnp.int32, (micro, 128), 1)
+        stat_out[m] = jnp.where(lanes < 64, mean, spread)
+        stat_copy(m).start()
+
+    def stage_b(m, sel):
+        floats = unslab(hid[m].astype(jnp.float32))
+        stat_copy(m).wait_recv()
+        mean_a, spread_a = stat_out[m, :, 0:1], stat_out[m, :, 64:65]
+        mean_b, spread_b = stat_in[m, :, 0:1], stat_in[m, :, 64:65]
+        mean = 0.5 * (mean_a + mean_b)
+        delta = mean_a - mean_b
+        var = (spread_a + spread_b + delta * delta * (0.5 * half)) / (2 * half)
+        scale = 1.0 + mods_ref[sel, 1:2, :]
+        shift = mods_ref[sel, 0:1, :]
+        normed = (floats - mean) * lax.rsqrt(var + 1e-06)
+        modded = (normed * scale + shift).astype(jnp.bfloat16)
+        for c in range(3):
+            @pl.when(m < 2)
+            def _():
+                pltpu.make_async_copy(wqv_ref.at[c], wq.at[m % 2, c], wq_sem.at[m % 2, c]).wait()
+
+            part = jnp.dot(modded, wq[sel, c], preferred_element_type=jnp.float32)
+            part_own[c] = part
+            part_out[m, c] = part.astype(jnp.bfloat16)
+            part_copy(m, c).start()
+
+    def stage_c(m, sel):
+        def take(c):
+            part_copy(m, c).wait_recv()
+            return part_own[c] + part_in[m, c].astype(jnp.float32)
+
+        def norm(value, gain):
+            pieces = []
+            for h in range(heads):
+                one = value[:, h * head_dim : (h + 1) * head_dim]
+                squares = jnp.mean(one * one, axis=-1, keepdims=True)
+                pieces.append((one * lax.rsqrt(squares + 1e-06) * gain).astype(jnp.bfloat16))
+            return pieces
+
+        @pl.when(m == 0)
+        def _():
+            pltpu.make_async_copy(stale_ref, kv, kv_sem.at[0]).wait()
+
+        @pl.when(m < 2)
+        def _():
+            pltpu.make_async_copy(wov_ref, wo.at[m % 2], wo_sem.at[m % 2]).wait()
+
+        queries = norm(take(0), gains_ref[sel, 0:1, :])
+        kv[0, m] = jnp.concatenate(norm(take(1), gains_ref[sel, 1:2, :]), axis=1)
+        kv[1, m] = take(2).astype(jnp.bfloat16)
+        bias = bias_ref[0:1, :]
+        outs = []
+        for h in range(heads):
+            cols = slice(h * head_dim, (h + 1) * head_dim)
+            keys = kv[0, :, :, cols].reshape(sections * micro, head_dim)
+            values = kv[1, :, :, cols].reshape(sections * micro, head_dim)
+            scores = lax.dot_general(
+                queries[h], keys, (((1,), (1,)), ((), ())), preferred_element_type=jnp.float32
+            )
+            scores = scores * inv_scale + bias
+            peak = jnp.max(scores, axis=-1, keepdims=True)
+            weights = jnp.exp(scores - peak)
+            total = jnp.sum(weights, axis=-1, keepdims=True)
+            mixed = jnp.dot(
+                weights.astype(jnp.bfloat16), values, preferred_element_type=jnp.float32
+            )
+            outs.append((mixed / total).astype(jnp.bfloat16))
+        attended = jnp.concatenate(outs, axis=1)
+        y = jnp.dot(attended, wo[sel], preferred_element_type=jnp.float32)
+        y = y.reshape(4, micro // 4, half)
+        y_own[...] = y
+        y_out[m] = y.astype(jnp.bfloat16)
+        for o in (2, 3, 1):
+            y_copy(m, o).start()
+
+    def stage_d(m, sel):
+        total = y_own[j]
+        for o in (1, 2, 3):
+            y_copy(m, o).wait_recv()
+            total = total + y_in[m, o - 1].astype(jnp.float32)
+        old = unslab(hid[m, pl.ds(2 * j, 2)].astype(jnp.float32))
+        new = old + mods_ref[sel, 2:3, :] * total
+        hnew[m] = slab(new).astype(jnp.bfloat16)
+
+        @pl.when(s < last)
+        def _():
+            for to in range(4):
+                next_copy(m, to).start()
+
+        @pl.when(s == last)
+        def _():
+            for e in range(2):
+                @pl.when(me != owner(m, e))
+                def _():
+                    out_copy(m, e).start()
+
+                @pl.when(me == owner(m, e))
+                def _():
+                    pltpu.make_async_copy(hnew.at[m, e], obuf.at[i], out_sem.at[i]).start()
+
+    stage_a(0)
+
+    @pl.loop(0, sections)
+    def _(m):
+        sel = jnp.minimum(m, 1)
+        stage_b(m, sel)
+        stage_c(m, sel)
+
+        @pl.when(m < last)
+        def _():
+            stage_a(m + 1)
+
+        stage_d(m, sel)
+
+    for k in range(8):
+        @pl.when(me != k)
+        def _():
+            init_copy(k).wait_send()
+
+    @pl.loop(0, sections)
+    def _(m):
+        stat_copy(m).wait_send()
+        for c in range(3):
+            part_copy(m, c).wait_send()
+        for o in (1, 2, 3):
+            y_copy(m, o).wait_send()
+
+        @pl.when(s < last)
+        def _():
+            for to in range(4):
+                next_copy(m, to).wait_send()
+
+        @pl.when(s == last)
+        def _():
+            for e in range(2):
+                @pl.when(me != owner(m, e))
+                def _():
+                    out_copy(m, e).wait_send()
+
+    for side in range(2):
+        pltpu.make_async_copy(obuf.at[side], obuf.at[side], out_sem.at[side]).wait()
+    out_ref[...] = obuf[...]
+
+
+def fused(
+    hidden_in, text_len, qkv_video, qkv_text, out_video, out_text, modulation, qk_gain, stale_kv
+):
+    sections = lax.axis_size("pipe")
+    section = lax.axis_index("pipe")
+    blk_index = lax.axis_index("blk")
+    rows, width = hidden_in.shape[1:]
+    half = width // 2
+    micro = rows * 8
+    dual_count = qkv_text.shape[0]
+    head_dim = qk_gain.shape[3]
+    local_width = stale_kv.shape[3]
+    heads = local_width // head_dim
+    dual = section < dual_count
+    chosen = jnp.minimum(section, dual_count - 1)
+    wqv = jnp.transpose(qkv_video[0], (1, 0, 2))
+    wqt = jnp.transpose(
+        lax.dynamic_index_in_dim(qkv_text, chosen, 0, keepdims=False), (1, 0, 2)
+    )
+    wot = lax.dynamic_index_in_dim(out_text, chosen, 0, keepdims=False)
+    mine = lax.dynamic_slice_in_dim(modulation[0], blk_index * half, half, 2)
+    mods = jnp.stack([jnp.where(dual, mine[1], mine[0]), mine[0]])
+    gains = qk_gain[0]
+    gains = jnp.stack([jnp.where(dual, gains[1], gains[0]), gains[0]])
+    places = jnp.arange(micro * sections, dtype=jnp.int32)
+    key_ok = (places >= micro) | (places < text_len[0])
+    bias = jnp.broadcast_to(jnp.where(key_ok, 0.0, -1e30).astype(jnp.float32), (8, places.size))
+    stale = stale_kv[0].reshape(2, sections, micro, local_width)
+    quarter = half // 2
+    hin = hidden_in[0].reshape(rows, 2, 2, quarter)
+    hin = jnp.transpose(hin, (1, 2, 0, 3)).reshape(2, 2 * rows, quarter)
+    bf16, f32 = jnp.bfloat16, jnp.float32
+    dma = pltpu.SemaphoreType.DMA
+    vmem = pl.BlockSpec(memory_space=pltpu.VMEM)
+    anyspace = pl.BlockSpec(memory_space=pl.ANY)
+    out = pl.pallas_call(
+        functools.partial(pipe_kernel, sections, dual_count, heads, head_dim),
+        out_shape=jax.ShapeDtypeStruct((2, 2 * rows, quarter), bf16),
+        in_specs=[vmem] * 4 + [anyspace] * 5,
+        out_specs=vmem,
+        scratch_shapes=[
+            pltpu.VMEM((sections, 8, 2 * rows, quarter), bf16),
+            pltpu.VMEM((sections, 2, 2 * rows, quarter), bf16),
+            pltpu.VMEM((2, 2 * rows, quarter), bf16),
+            pltpu.VMEM((sections, micro, 128), f32),
+            pltpu.VMEM((sections, micro, 128), f32),
+            pltpu.VMEM((3, micro, local_width), f32),
+            pltpu.VMEM((sections, 3, micro, local_width), bf16),
+            pltpu.VMEM((sections, 3, micro, local_width), bf16),
+            pltpu.VMEM((4, micro // 4, half), f32),
+            pltpu.VMEM((sections, 4, micro // 4, half), bf16),
+            pltpu.VMEM((sections, 3, micro // 4, half), bf16),
+            pltpu.VMEM((2, 3, half, local_width), bf16),
+            pltpu.VMEM((2, local_width, half), bf16),
+            pltpu.VMEM((2, sections, micro, local_width), bf16),
+            dma((8,)),
+            dma((sections, 8)),
+            dma((sections,)),
+            dma((sections,)),
+            dma((sections, 3)),
+            dma((sections, 3)),
+            dma((sections, 3)),
+            dma((sections, 3)),
+            dma((sections, 4)),
+            dma((2,)),
+            dma((2, 3)),
+            dma((2,)),
+            dma((1,)),
+        ],
+        compiler_params=pltpu.CompilerParams(
+            collective_id=0, has_side_effects=True, vmem_limit_bytes=40 * 1024 * 1024
+        ),
+        cost_estimate=pl.CostEstimate(
+            flops=8 * micro * sections * half * local_width,
+            bytes_accessed=16 * half * local_width,
+            transcendentals=heads * micro * sections * micro * sections,
+        ),
+    )(bias, hin, mods, gains, wqv, wqt, out_video[0], wot, stale)
+    out = out.reshape(2, 2, rows, quarter)
+    return jnp.transpose(out, (2, 0, 1, 3)).reshape(1, rows, width)
 
 
 def from_behind(shard, axis, by):
@@ -137,8 +511,10 @@
 
 
 def solution(mesh):
+    shape = mesh.shape
+    small = shape["blk"] == 2 and shape["uly"] == 4 and shape["pipe"] == 4
     return jax.shard_map(
-        local,
+        fused if small else local,
         mesh=mesh,
         in_specs=(
             P("pipe", ("blk", "uly"), None),

time: 641 us -> 128 us (0.20); the launches traced: 630 us -> 128 us
  waiting for transfers between devices: 373 us -> 0 us
  Pallas kernels: 0 us -> 120 us
  blocking collectives: 97.6 us -> 0 us
  matrix products: 55.1 us -> 0 us
  starting transfers between devices: 35.8 us -> 0 us
  local copies, waits for them, and re-layouts: 36.4 us -> 5.8 us
  other arithmetic: 15.9 us -> 0.74 us
  between operations: 16 us -> 0.9 us
    all_gather x4 -> x0, waiting for transfers between devices: 223 us -> none  [the longest x1 90.8 us: local(): lax.all_gather(qkv_video[0], 'blk', axis=0, tiled=True)]
    reduce_scatter x7 -> x0, waiting for transfers between devices: 127 us -> none  [local(): lax.psum_scatter(partial_value, 'uly', scatter_dimension=0, tiled=True)]
    pallas_call x0 -> x1, Pallas kernels: none -> 120 us  [fused(): pl.pallas_call(functools.partial(pipe_kernel, sections, dual_count, heads...]
    all_gather x21 -> x0, blocking collectives: 97.6 us -> none  [the longest x7 49.9 us: local(): gathered = lax.all_gather(modded, 'uly', axis=0, tiled=True)]
    dot_general x21 -> x0, matrix products: 52.8 us -> none  [the longest x7 36.2 us: local(): jnp.dot(operand, video_proj, preferred_element_type=jnp.float32)]
    ppermute x18 -> x0, starting transfers between devices: 35.4 us -> none  [from_behind(): return lax.ppermute(shard, axis, pairs)]
    ppermute x18 -> x0, waiting for transfers between devices: 22.2 us -> none  [from_behind(): return lax.ppermute(shard, axis, pairs)]
    unnamed x57 -> x12, local copies, waits for them, and re-layouts: 17.8 us -> 1.57 us
  transfers between devices with their start and end apart: 29 -> 0, of which waited for: 18 -> 0; matrix products, arithmetic and copies ran while one was open for 4% -> 0% of each run, Pallas kernels for 0% -> 0%
where the time goes in v1:
time: 128 us
  Pallas kernels  120 us (94%)
  local copies, waits for them, and re-layouts  5.8 us (5%)
    pallas_call x1, Pallas kernels, fused(): pl.pallas_call(functools.partial(pipe_kernel, sections, dual_count, heads...  120 us

profile of v1, /device:TPU:25, one launch (start us, length us, event | category | flops | bytes accessed | tf_op | source)
XLA Modules:
  0.0 127.7 jit_solution(14958245719957299969)
XLA Ops:
  0.0 0.0 copy-start
  0.8 0.7 slice_bitcast_fusion
  1.5 0.7 bitcast_select_fusion
  2.2 0.9 constant_dynamic-slice_fusion
  3.2 0.0 copy-done
  3.2 0.1 dynamic-slice_bitcast_fusion.1.wot_ref
  3.3 0.0 copy-start.1
  3.3 0.0 copy-start.2
  3.3 0.0 copy-start.3
  3.4 0.0 copy-start.4
  3.4 2.5 %dynamic-slice_bitcast_fusion.wqt_ref = bf16[3,1536,384]{2,1,0:T(8,128)(2,1)S(1)} fusion(bf16[2,1536,3,384]{3,1,2,0:T(8,128)(2,1)} %param.12, s32[]{:T(128)S(6)} %select_n.49), kind=kLoop, calls=%fused_computation | loop fusion | bytes 7077892 | tf_op jit(solution)/shard_map/transpose | solution.py:317
  5.9 0.5 copy-done.1
  6.4 0.3 copy-done.2
  6.7 0.1 copy-done.3
  6.8 0.0 copy-done.4
  6.8 120.3 %shard_map.91 = bf16[2,16,768]{2,1,0:T(8,128)(2,1)S(1)} custom-call(f32[8,256]{1,0:T(8,128)S(1)} %broadcast_in_dim.13.bias_ref, bf16[2,16,768]{2,1,0:T(8,128)(2,1)S(1)} %bitcast.42, f32[2,3,1536]{2,1,0:T(4,128)S(1)} %pad_maximum_fusion.mods_ref, f32[2,2,128]{2,1,0:T(2,128)S(1)} %pad_maximum_fusion.1.gains_ref, bf16[3,1536,384]{2,1,0:T(8,128)(2,1)S(1)} %bitcast.38, ...), custom_call_target="tpu_custom_call" | custom-call | flops 1207959552 | bytes 9437184 | tf_op jit(solution)/shard_map/pallas_call | solution.py:336
  127.1 0.6 copy.23
  (6 shorter events, 0.0 us)
Async XLA Ops:
  0.0 3.2 %copy-start = (bf16[2,384,1536]{2,1,0:T(8,128)(2,1)S(1)}, bf16[2,384,1536]{2,1,0:T(8,128)(2,1)}, u32[]{:S(2)}) copy-start(bf16[2,384,1536]{2,1,0:T(8,128)(2,1)} %param.14) | copy-start | bytes 7077892
  3.3 3.1 %copy-start.1 = (bf16[1,1536,3,384]{3,1,2,0:T(8,128)(2,1)S(1)}, bf16[1,1536,3,384]{3,1,2,0:T(8,128)(2,1)}, u32[]{:S(2)}) copy-start(bf16[1,1536,3,384]{3,1,2,0:T(8,128)(2,1)} %param.11) | copy-start | bytes 10616836
  3.3 3.4 %copy-start.2 = (bf16[1,384,1536]{2,1,0:T(8,128)(2,1)S(1)}, bf16[1,384,1536]{2,1,0:T(8,128)(2,1)}, u32[]{:S(2)}) copy-start(bf16[1,384,1536]{2,1,0:T(8,128)(2,1)} %param.13) | copy-start | bytes 3538948
  3.3 3.5 %copy-start.3 = (bf16[1,2,256,384]{3,2,1,0:T(8,128)(2,1)S(1)}, bf16[1,2,256,384]{3,2,1,0:T(8,128)(2,1)}, u32[]{:S(2)}) copy-start(bf16[1,2,256,384]{3,2,1,0:T(8,128)(2,1)} %param.17) | copy-start | bytes 1179652
  3.4 3.4 %copy-start.4 = (bf16[1,8,3072]{2,1,0:T(8,128)(2,1)S(1)}, bf16[1,8,3072]{2,1,0:T(8,128)(2,1)}, u32[]{:S(2)}) copy-start(bf16[1,8,3072]{2,1,0:T(8,128)(2,1)} %param.9) | copy-start | bytes 147460

commit v2 on v1

--- a/solution.py
+++ b/solution.py
@@ -25,11 +25,11 @@
 
 def pipe_kernel(
     sections, dual_count, heads, head_dim,
-    bias_ref, hin_ref, mods_ref, gains_ref, wqv_ref, wqt_ref, wov_ref, wot_ref, stale_ref,
+    len_ref, hin_ref, mod_ref, gain_ref, wqv_ref, wqt_ref, wov_ref, wot_ref, stale_ref,
     out_ref,
-    hid, hnew, obuf, stat_out, stat_in, part_own, part_out, part_in, y_own, y_out, y_in,
+    mods, gains, hid, hnew, obuf, stat_first, stat_out, stat_in, part_own, part_out, part_in, y_own, y_out, y_in,
     wq, wo, kv,
-    init_sem, hid_sem, stat_ssem, stat_rsem, part_ssem, part_rsem, y_ssem, y_rsem,
+    init_sem, hid_sem, fwd_sem, first_sem, stat_ssem, stat_rsem, part_ssem, part_rsem, y_ssem, y_rsem,
     next_sem, out_sem, wq_sem, wo_sem, kv_sem,
 ):
     s = lax.axis_index("pipe")
@@ -37,23 +37,32 @@
     j = lax.axis_index("uly")
     me = (s * 2 + i) * 4 + j
     local_width = heads * head_dim
-    half = mods_ref.shape[2]
+    half = mods.shape[2]
     micro = 64
     inv_scale = 1.0 / math.sqrt(head_dim)
     last = sections - 1
 
+    chosen = jnp.minimum(s, dual_count - 1)
+    edges = list(range(0, 3 * local_width, 256)) + [3 * local_width]
+    chunks = list(zip(edges[:-1], edges[1:]))
+
+    def weight_copy(source, slot, c):
+        return pltpu.make_async_copy(
+            source, wq.at[slot, :, pl.ds(c * local_width, local_width)], wq_sem.at[slot, c]
+        )
+
     for c in range(3):
         @pl.when(s < dual_count)
         def _():
-            pltpu.make_async_copy(wqt_ref.at[c], wq.at[0, c], wq_sem.at[0, c]).start()
+            weight_copy(wqt_ref.at[chosen, c], 0, c).start()
 
         @pl.when(s >= dual_count)
         def _():
-            pltpu.make_async_copy(wqv_ref.at[c], wq.at[0, c], wq_sem.at[0, c]).start()
+            weight_copy(wqv_ref.at[c], 0, c).start()
 
     @pl.when(s < dual_count)
     def _():
-        pltpu.make_async_copy(wot_ref, wo.at[0], wo_sem.at[0]).start()
+        pltpu.make_async_copy(wot_ref.at[chosen], wo.at[0], wo_sem.at[0]).start()
 
     @pl.when(s >= dual_count)
     def _():
@@ -61,7 +70,7 @@
 
     pltpu.make_async_copy(stale_ref, kv, kv_sem.at[0]).start()
     for c in range(3):
-        pltpu.make_async_copy(wqv_ref.at[c], wq.at[1, c], wq_sem.at[1, c]).start()
+        weight_copy(wqv_ref.at[c], 1, c).start()
     pltpu.make_async_copy(wov_ref, wo.at[1], wo_sem.at[1]).start()
 
     barrier = pltpu.get_barrier_semaphore()
@@ -74,6 +83,29 @@
             pl.semaphore_signal(
                 barrier, inc=1, device_id=(d // 8, (d // 4) % 2, d % 4), device_id_type=MESH
             )
+
+    dual = s < dual_count
+    cols = pl.ds(pl.multiple_of(i * half, 128), half)
+    for k in range(3):
+        video, text = mod_ref[k, 0:1, cols], mod_ref[k, 1:2, cols]
+        mods[0, k : k + 1, :] = jnp.where(dual, text, video)
+        mods[1, k : k + 1, :] = video
+    gains[1] = gain_ref[0]
+    gains[0] = jnp.where(dual, gain_ref[1], gain_ref[0])
+
+    def stats_of(floats):
+        mean = jnp.mean(floats, axis=-1, keepdims=True)
+        centred = floats - mean
+        spread = jnp.sum(centred * centred, axis=-1, keepdims=True)
+        return mean, spread
+
+    def packed_stats(floats):
+        mean, spread = stats_of(floats)
+        lanes = lax.broadcasted_iota(jnp.int32, (floats.shape[0], 128), 1)
+        return jnp.where(lanes < 64, mean, spread).reshape(-1, 8, 128)
+
+    for side in range(2):
+        stat_first[side] = packed_stats(unslab(hin_ref[side : side + 1].astype(jnp.float32)))[0]
 
     pl.semaphore_wait(barrier, devices - 1)
 
@@ -87,44 +119,70 @@
             device_id_type=MESH,
         )
 
+    def first_copy(k):
+        return pltpu.make_async_remote_copy(
+            src_ref=stat_first.at[1 - k // 4],
+            dst_ref=stat_in.at[s, i * 4 + j],
+            send_sem=first_sem.at[k],
+            recv_sem=stat_rsem.at[s, i * 4 + j],
+            device_id=(0, k // 4, k % 4),
+            device_id_type=MESH,
+        )
+
     for k in range(8):
         @pl.when(me != k)
         def _():
             init_copy(k).start()
+            first_copy(k).start()
 
         @pl.when(me == k)
         def _():
             pltpu.make_async_copy(
                 hin_ref.at[k // 4], hid.at[s, i * 4 + j], hid_sem.at[s, i * 4 + j]
             ).start()
-
-    def stat_copy(m):
-        return pltpu.make_async_remote_copy(
-            src_ref=stat_out.at[m], dst_ref=stat_in.at[m],
-            send_sem=stat_ssem.at[m], recv_sem=stat_rsem.at[m],
-            device_id=(s, 1 - i, j), device_id_type=MESH,
+            pltpu.make_async_copy(
+                stat_first.at[1 - k // 4], stat_in.at[s, i * 4 + j], stat_rsem.at[s, i * 4 + j]
+            ).start()
+
+    def stat_copy(m, to):
+        return pltpu.make_async_remote_copy(
+            src_ref=stat_out.at[m], dst_ref=stat_in.at[m, pl.ds(2 * j, 2)],
+            send_sem=stat_ssem.at[m, to], recv_sem=stat_rsem.at[m, j],
+            device_id=(s + 1, 1 - i, to), device_id_type=MESH,
         )
 
     def part_copy(m, c):
         return pltpu.make_async_remote_copy(
-            src_ref=part_out.at[m, c], dst_ref=part_in.at[m, c],
+            src_ref=part_out.at[m, :, pl.ds(chunks[c][0], chunks[c][1] - chunks[c][0])],
+            dst_ref=part_in.at[m, :, pl.ds(chunks[c][0], chunks[c][1] - chunks[c][0])],
             send_sem=part_ssem.at[m, c], recv_sem=part_rsem.at[m, c],
             device_id=(s, 1 - i, j), device_id_type=MESH,
         )
 
-    def y_copy(m, o):
+    def y_copy(m, o, e):
         to = (j + o) % 4
-        return pltpu.make_async_remote_copy(
-            src_ref=y_out.at[m, to], dst_ref=y_in.at[m, o - 1],
-            send_sem=y_ssem.at[m, o - 1], recv_sem=y_rsem.at[m, o - 1],
+        slot = 2 * (o - 1) + e
+        return pltpu.make_async_remote_copy(
+            src_ref=y_out.at[m, 2 * to + e], dst_ref=y_in.at[m, slot],
+            send_sem=y_ssem.at[m, slot], recv_sem=y_rsem.at[m, slot],
             device_id=(s, i, to), device_id_type=MESH,
         )
 
-    def next_copy(m, to):
-        return pltpu.make_async_remote_copy(
-            src_ref=hnew.at[m], dst_ref=hid.at[m, pl.ds(2 * j, 2)],
-            send_sem=next_sem.at[m, to], recv_sem=hid_sem.at[m, j],
-            device_id=(s + 1, i, to), device_id_type=MESH,
+    parity = j % 2
+
+    def next_copy(m, e, side):
+        return pltpu.make_async_remote_copy(
+            src_ref=hnew.at[m, e], dst_ref=hid.at[m, 2 * j + e],
+            send_sem=next_sem.at[m, 2 * e + side], recv_sem=hid_sem.at[m, 2 * j + e],
+            device_id=(s + 1, i, 2 * side + parity), device_id_type=MESH,
+        )
+
+    def forward_copy(m, e, side):
+        g = 2 * (2 * side + parity) + e
+        return pltpu.make_async_remote_copy(
+            src_ref=hid.at[m, g], dst_ref=hid.at[m, g],
+            send_sem=fwd_sem.at[m, 2 * e + side], recv_sem=hid_sem.at[m, g],
+            device_id=(s, i, j + 1 - 2 * parity), device_id_type=MESH,
         )
 
     def out_copy(m, e):
@@ -138,52 +196,63 @@
     def owner(m, e):
         return m * 8 + 2 * j + e
 
-    def stage_a(m):
+    def arrive(m):
+        def take(ref, sem):
+            pltpu.make_async_copy(ref, ref, sem).wait()
+
         @pl.when(s == 0)
         def _():
             for r in range(8):
-                pltpu.make_async_copy(hid.at[m, r], hid.at[m, r], hid_sem.at[m, r]).wait()
+                take(hid.at[m, r], hid_sem.at[m, r])
+                take(stat_in.at[m, r], stat_rsem.at[m, r])
 
         @pl.when(s > 0)
         def _():
+            for e in range(2):
+                for side in range(2):
+                    g = 2 * (2 * side + parity) + e
+                    take(hid.at[m, g], hid_sem.at[m, g])
+                    forward_copy(m, e, side).start()
+            for e in range(2):
+                for side in range(2):
+                    g = 2 * (2 * side + 1 - parity) + e
+                    take(hid.at[m, g], hid_sem.at[m, g])
             for r in range(4):
-                pair = hid.at[m, pl.ds(2 * r, 2)]
-                pltpu.make_async_copy(pair, pair, hid_sem.at[m, r]).wait()
-
+                take(stat_in.at[m, pl.ds(2 * r, 2)], stat_rsem.at[m, r])
+
+    def stage_b(m, sel):
+        arrive(m)
         floats = unslab(hid[m].astype(jnp.float32))
-        mean = jnp.mean(floats, axis=-1, keepdims=True)
-        centred = floats - mean
-        spread = jnp.sum(centred * centred, axis=-1, keepdims=True)
-        lanes = lax.broadcasted_iota(jnp.int32, (micro, 128), 1)
-        stat_out[m] = jnp.where(lanes < 64, mean, spread)
-        stat_copy(m).start()
-
-    def stage_b(m, sel):
-        floats = unslab(hid[m].astype(jnp.float32))
-        stat_copy(m).wait_recv()
-        mean_a, spread_a = stat_out[m, :, 0:1], stat_out[m, :, 64:65]
-        mean_b, spread_b = stat_in[m, :, 0:1], stat_in[m, :, 64:65]
+        mean_a, spread_a = stats_of(floats)
+        other = stat_in[m].reshape(micro, 128)
+        mean_b, spread_b = other[:, 0:1], other[:, 64:65]
         mean = 0.5 * (mean_a + mean_b)
         delta = mean_a - mean_b
         var = (spread_a + spread_b + delta * delta * (0.5 * half)) / (2 * half)
-        scale = 1.0 + mods_ref[sel, 1:2, :]
-        shift = mods_ref[sel, 0:1, :]
+        scale = 1.0 + mods[sel, 1:2, :]
+        shift = mods[sel, 0:1, :]
         normed = (floats - mean) * lax.rsqrt(var + 1e-06)
         modded = (normed * scale + shift).astype(jnp.bfloat16)
-        for c in range(3):
-            @pl.when(m < 2)
-            def _():
-                pltpu.make_async_copy(wqv_ref.at[c], wq.at[m % 2, c], wq_sem.at[m % 2, c]).wait()
-
-            part = jnp.dot(modded, wq[sel, c], preferred_element_type=jnp.float32)
-            part_own[c] = part
-            part_out[m, c] = part.astype(jnp.bfloat16)
+
+        @pl.when(m < 2)
+        def _():
+            for c in range(3):
+                weight_copy(wqv_ref.at[c], sel, c).wait()
+
+        for c, (lo, hi) in enumerate(chunks):
+            part = jnp.dot(modded, wq[sel, :, lo:hi], preferred_element_type=jnp.float32)
+            part_own[m % 2, :, lo:hi] = part
+            part_out[m, :, lo:hi] = part.astype(jnp.bfloat16)
             part_copy(m, c).start()
 
     def stage_c(m, sel):
+        early = [c for c in range(len(chunks)) if chunks[c][0] < 2 * local_width]
+        for c in early:
+            part_copy(m, c).wait_recv()
+
         def take(c):
-            part_copy(m, c).wait_recv()
-            return part_own[c] + part_in[m, c].astype(jnp.float32)
+            lo, hi = c * local_width, (c + 1) * local_width
+            return part_own[m % 2, :, lo:hi] + part_in[m, :, lo:hi].astype(jnp.float32)
 
         def norm(value, gain):
             pieces = []
@@ -199,17 +268,16 @@
 
         @pl.when(m < 2)
         def _():
-            pltpu.make_async_copy(wov_ref, wo.at[m % 2], wo_sem.at[m % 2]).wait()
-
-        queries = norm(take(0), gains_ref[sel, 0:1, :])
-        kv[0, m] = jnp.concatenate(norm(take(1), gains_ref[sel, 1:2, :]), axis=1)
-        kv[1, m] = take(2).astype(jnp.bfloat16)
-        bias = bias_ref[0:1, :]
-        outs = []
+            pltpu.make_async_copy(wov_ref, wo.at[sel], wo_sem.at[sel]).wait()
+
+        queries = norm(take(0), gains[sel, 0:1, :])
+        kv[0, m] = jnp.concatenate(norm(take(1), gains[sel, 1:2, :]), axis=1)
+        places = lax.broadcasted_iota(jnp.int32, (1, sections * micro), 1)
+        bias = jnp.where((places >= micro) | (places < len_ref[0]), 0.0, -1e30)
+        raised = []
         for h in range(heads):
             cols = slice(h * head_dim, (h + 1) * head_dim)
             keys = kv[0, :, :, cols].reshape(sections * micro, head_dim)
-            values = kv[1, :, :, cols].reshape(sections * micro, head_dim)
             scores = lax.dot_general(
                 queries[h], keys, (((1,), (1,)), ((), ())), preferred_element_type=jnp.float32
             )
@@ -217,35 +285,42 @@
             peak = jnp.max(scores, axis=-1, keepdims=True)
             weights = jnp.exp(scores - peak)
             total = jnp.sum(weights, axis=-1, keepdims=True)
-            mixed = jnp.dot(
-                weights.astype(jnp.bfloat16), values, preferred_element_type=jnp.float32
-            )
+            raised.append((weights.astype(jnp.bfloat16), total))
+        for c in range(len(early), len(chunks)):
+            part_copy(m, c).wait_recv()
+        kv[1, m] = take(2).astype(jnp.bfloat16)
+        outs = []
+        for h, (weights, total) in enumerate(raised):
+            cols = slice(h * head_dim, (h + 1) * head_dim)
+            values = kv[1, :, :, cols].reshape(sections * micro, head_dim)
+            mixed = jnp.dot(weights, values, preferred_element_type=jnp.float32)
             outs.append((mixed / total).astype(jnp.bfloat16))
         attended = jnp.concatenate(outs, axis=1)
-        y = jnp.dot(attended, wo[sel], preferred_element_type=jnp.float32)
-        y = y.reshape(4, micro // 4, half)
+        y = slab(jnp.dot(attended, wo[sel], preferred_element_type=jnp.float32))
         y_own[...] = y
         y_out[m] = y.astype(jnp.bfloat16)
-        for o in (2, 3, 1):
-            y_copy(m, o).start()
+        for e in range(2):
+            for o in (2, 3, 1):
+                y_copy(m, o, e).start()
 
     def stage_d(m, sel):
-        total = y_own[j]
-        for o in (1, 2, 3):
-            y_copy(m, o).wait_recv()
-            total = total + y_in[m, o - 1].astype(jnp.float32)
-        old = unslab(hid[m, pl.ds(2 * j, 2)].astype(jnp.float32))
-        new = old + mods_ref[sel, 2:3, :] * total
-        hnew[m] = slab(new).astype(jnp.bfloat16)
-
-        @pl.when(s < last)
-        def _():
-            for to in range(4):
-                next_copy(m, to).start()
-
-        @pl.when(s == last)
-        def _():
-            for e in range(2):
+        gate = mods[sel, 2:3, :]
+        gate = slab(jnp.broadcast_to(gate, (8, half)))[0]
+        for e in range(2):
+            total = y_own[2 * j + e]
+            for o in (1, 2, 3):
+                y_copy(m, o, e).wait_recv()
+                total = total + y_in[m, 2 * (o - 1) + e].astype(jnp.float32)
+            old = hid[m, 2 * j + e].astype(jnp.float32)
+            hnew[m, e] = (old + gate * total).astype(jnp.bfloat16)
+
+            @pl.when(s < last)
+            def _():
+                for side in range(2):
+                    next_copy(m, e, side).start()
+
+            @pl.when(s == last)
+            def _():
                 @pl.when(me != owner(m, e))
                 def _():
                     out_copy(m, e).start()
@@ -254,17 +329,22 @@
                 def _():
                     pltpu.make_async_copy(hnew.at[m, e], obuf.at[i], out_sem.at[i]).start()
 
-    stage_a(0)
+        @pl.when(s < last)
+        def _():
+            stat_out[m] = packed_stats(unslab(hnew[m].astype(jnp.float32)))
+            for to in range(4):
+                stat_copy(m, to).start()
+
+    stage_b(0, 0)
 
     @pl.loop(0, sections)
     def _(m):
         sel = jnp.minimum(m, 1)
-        stage_b(m, sel)
         stage_c(m, sel)
 
         @pl.when(m < last)
         def _():
-            stage_a(m + 1)
+            stage_b(m + 1, 1)
 
         stage_d(m, sel)
 
@@ -272,19 +352,29 @@
         @pl.when(me != k)
         def _():
             init_copy(k).wait_send()
+            first_copy(k).wait_send()
 
     @pl.loop(0, sections)
     def _(m):
-        stat_copy(m).wait_send()
-        for c in range(3):
+        for c in range(len(chunks)):
             part_copy(m, c).wait_send()
-        for o in (1, 2, 3):
-            y_copy(m, o).wait_send()
+        for e in range(2):
+            for o in (1, 2, 3):
+                y_copy(m, o, e).wait_send()
+
+        @pl.when(s > 0)
+        def _():
+            for e in range(2):
+                for side in range(2):
+                    forward_copy(m, e, side).wait_send()
 
         @pl.when(s < last)
         def _():
+            for e in range(2):
+                for side in range(2):
+                    next_copy(m, e, side).wait_send()
             for to in range(4):
-                next_copy(m, to).wait_send()
+                stat_copy(m, to).wait_send()
 
         @pl.when(s == last)
         def _():
@@ -302,8 +392,6 @@
     hidden_in, text_len, qkv_video, qkv_text, out_video, out_text, modulation, qk_gain, stale_kv
 ):
     sections = lax.axis_size("pipe")
-    section = lax.axis_index("pipe")
-    blk_index = lax.axis_index("blk")
     rows, width = hidden_in.shape[1:]
     half = width // 2
     micro = rows * 8
@@ -311,24 +399,14 @@
     head_dim = qk_gain.shape[3]
     local_width = stale_kv.shape[3]
     heads = local_width // head_dim
-    dual = section < dual_count
-    chosen = jnp.minimum(section, dual_count - 1)
     wqv = jnp.transpose(qkv_video[0], (1, 0, 2))
-    wqt = jnp.transpose(
-        lax.dynamic_index_in_dim(qkv_text, chosen, 0, keepdims=False), (1, 0, 2)
-    )
-    wot = lax.dynamic_index_in_dim(out_text, chosen, 0, keepdims=False)
-    mine = lax.dynamic_slice_in_dim(modulation[0], blk_index * half, half, 2)
-    mods = jnp.stack([jnp.where(dual, mine[1], mine[0]), mine[0]])
-    gains = qk_gain[0]
-    gains = jnp.stack([jnp.where(dual, gains[1], gains[0]), gains[0]])
-    places = jnp.arange(micro * sections, dtype=jnp.int32)
-    key_ok = (places >= micro) | (places < text_len[0])
-    bias = jnp.broadcast_to(jnp.where(key_ok, 0.0, -1e30).astype(jnp.float32), (8, places.size))
+    wqt = jnp.transpose(qkv_text, (0, 2, 1, 3))
+    mods = jnp.transpose(modulation[0], (1, 0, 2))
     stale = stale_kv[0].reshape(2, sections, micro, local_width)
     quarter = half // 2
     hin = hidden_in[0].reshape(rows, 2, 2, quarter)
     hin = jnp.transpose(hin, (1, 2, 0, 3)).reshape(2, 2 * rows, quarter)
+    pieces = -(-3 * local_width // 256)
     bf16, f32 = jnp.bfloat16, jnp.float32
     dma = pltpu.SemaphoreType.DMA
     vmem = pl.BlockSpec(memory_space=pltpu.VMEM)
@@ -336,31 +414,36 @@
     out = pl.pallas_call(
         functools.partial(pipe_kernel, sections, dual_count, heads, head_dim),
         out_shape=jax.ShapeDtypeStruct((2, 2 * rows, quarter), bf16),
-        in_specs=[vmem] * 4 + [anyspace] * 5,
+        in_specs=[pl.BlockSpec(memory_space=pltpu.SMEM)] + [vmem] * 3 + [anyspace] * 5,
         out_specs=vmem,
         scratch_shapes=[
+            pltpu.VMEM((2, 3, half), f32),
+            pltpu.VMEM((2, 2, head_dim), f32),
             pltpu.VMEM((sections, 8, 2 * rows, quarter), bf16),
             pltpu.VMEM((sections, 2, 2 * rows, quarter), bf16),
             pltpu.VMEM((2, 2 * rows, quarter), bf16),
-            pltpu.VMEM((sections, micro, 128), f32),
-            pltpu.VMEM((sections, micro, 128), f32),
-            pltpu.VMEM((3, micro, local_width), f32),
-            pltpu.VMEM((sections, 3, micro, local_width), bf16),
-            pltpu.VMEM((sections, 3, micro, local_width), bf16),
-            pltpu.VMEM((4, micro // 4, half), f32),
-            pltpu.VMEM((sections, 4, micro // 4, half), bf16),
-            pltpu.VMEM((sections, 3, micro // 4, half), bf16),
-            pltpu.VMEM((2, 3, half, local_width), bf16),
+            pltpu.VMEM((2, 8, 128), f32),
+            pltpu.VMEM((sections, 2, 8, 128), f32),
+            pltpu.VMEM((sections, 8, 8, 128), f32),
+            pltpu.VMEM((2, micro, 3 * local_width), f32),
+            pltpu.VMEM((sections, micro, 3 * local_width), bf16),
+            pltpu.VMEM((sections, micro, 3 * local_width), bf16),
+            pltpu.VMEM((8, 2 * rows, quarter), f32),
+            pltpu.VMEM((sections, 8, 2 * rows, quarter), bf16),
+            pltpu.VMEM((sections, 6, 2 * rows, quarter), bf16),
+            pltpu.VMEM((2, half, 3 * local_width), bf16),
             pltpu.VMEM((2, local_width, half), bf16),
             pltpu.VMEM((2, sections, micro, local_width), bf16),
             dma((8,)),
             dma((sections, 8)),
-            dma((sections,)),
-            dma((sections,)),
-            dma((sections, 3)),
-            dma((sections, 3)),
-            dma((sections, 3)),
-            dma((sections, 3)),
+            dma((sections, 4)),
+            dma((8,)),
+            dma((sections, 4)),
+            dma((sections, 8)),
+            dma((sections, pieces)),
+            dma((sections, pieces)),
+            dma((sections, 6)),
+            dma((sections, 6)),
             dma((sections, 4)),
             dma((2,)),
             dma((2, 3)),
@@ -368,14 +451,14 @@
             dma((1,)),
         ],
         compiler_params=pltpu.CompilerParams(
-            collective_id=0, has_side_effects=True, vmem_limit_bytes=40 * 1024 * 1024
+            collective_id=0, has_side_effects=True, vmem_limit_bytes=60 * 1024 * 1024
         ),
         cost_estimate=pl.CostEstimate(
             flops=8 * micro * sections * half * local_width,
             bytes_accessed=16 * half * local_width,
             transcendentals=heads * micro * sections * micro * sections,
         ),
-    )(bias, hin, mods, gains, wqv, wqt, out_video[0], wot, stale)
+    )(text_len, hin, mods, qk_gain[0], wqv, wqt, out_video[0], out_text, stale)
     out = out.reshape(2, 2, rows, quarter)
     return jnp.transpose(out, (2, 0, 1, 3)).reshape(1, rows, width)
 

time: 128 us -> 106 us (0.83)
  Pallas kernels: 120 us -> 104 us
  local copies, waits for them, and re-layouts: 5.8 us -> 1.42 us
    pallas_call x1, Pallas kernels: 120 us -> 104 us  [fused(): pl.pallas_call(functools.partial(pipe_kernel, sections, dual_count, heads...]
    transpose x1 -> x0, local copies, waits for them, and re-layouts: 2.51 us -> none  [fused(): jnp.transpose(lax.dynamic_index_in_dim(qkv_text, chosen, 0, keepdims=Fals...]
where the time goes in v2:
time: 106 us
  Pallas kernels  104 us (98%)
  local copies, waits for them, and re-layouts  1.42 us (1%)
    pallas_call x1, Pallas kernels, fused(): pl.pallas_call(functools.partial(pipe_kernel, sections, dual_count, heads...  104 us

profile of v2, /device:TPU:25, one launch (start us, length us, event | category | flops | bytes accessed | tf_op | source)
XLA Modules:
  0.0 106.0 jit_solution(440234208595393275)
XLA Ops:
  0.7 104.0 %shard_map.91 = bf16[2,16,768]{2,1,0:T(8,128)(2,1)} custom-call(s32[1]{0:T(128)S(6)} %copy.11.len_ref, bf16[2,16,768]{2,1,0:T(8,128)(2,1)} %bitcast.26, f32[3,2,3072]{2,1,0:T(2,128)} %bitcast.25, f32[2,2,128]{2,1,0:T(2,128)} %bitcast.27, bf16[3,1536,384]{2,1,0:T(8,128)(2,1)} %bitcast.21, bf16[2,3,1536,384]{3,2,1,0:T(8,128)(2,1)} %bitcast.20, ...), custom_call_target="tpu_custom_call" | custom-call | flops 1207959552 | bytes 9437184 | tf_op jit(solution)/shard_map/pallas_call | solution.py:414
  104.6 1.4 %copy.12 = bf16[1,8,3072]{2,1,0:T(8,128)(2,1)} copy(bf16[1,8,3072]{2,1,0:T(8,128)(2,1)} %bitcast.24) | data formatting | bytes 98304

commit v3 on v2

--- a/solution.py
+++ b/solution.py
@@ -42,8 +42,17 @@
     inv_scale = 1.0 / math.sqrt(head_dim)
     last = sections - 1
 
+    barrier = pltpu.get_barrier_semaphore()
+    devices = sections * 8
+    for d in range(devices):
+        @pl.when(d != me)
+        def _():
+            pl.semaphore_signal(
+                barrier, inc=1, device_id=(d // 8, (d // 4) % 2, d % 4), device_id_type=MESH
+            )
+
     chosen = jnp.minimum(s, dual_count - 1)
-    edges = list(range(0, 3 * local_width, 256)) + [3 * local_width]
+    edges = [0, 256, 2 * local_width, 3 * local_width]
     chunks = list(zip(edges[:-1], edges[1:]))
 
     def weight_copy(source, slot, c):
@@ -72,17 +81,6 @@
     for c in range(3):
         weight_copy(wqv_ref.at[c], 1, c).start()
     pltpu.make_async_copy(wov_ref, wo.at[1], wo_sem.at[1]).start()
-
-    barrier = pltpu.get_barrier_semaphore()
-    devices = sections * 8
-
-    @pl.loop(0, devices)
-    def _(d):
-        @pl.when(d != me)
-        def _():
-            pl.semaphore_signal(
-                barrier, inc=1, device_id=(d // 8, (d // 4) % 2, d % 4), device_id_type=MESH
-            )
 
     dual = s < dual_count
     cols = pl.ds(pl.multiple_of(i * half, 128), half)
@@ -109,13 +107,16 @@
 
     pl.semaphore_wait(barrier, devices - 1)
 
+    def init_target(k):
+        return 4 * (k // 2) + 2 * (k % 2) + j // 2
+
     def init_copy(k):
         return pltpu.make_async_remote_copy(
-            src_ref=hin_ref.at[k // 4],
+            src_ref=hin_ref.at[k // 2],
             dst_ref=hid.at[s, i * 4 + j],
             send_sem=init_sem.at[k],
             recv_sem=hid_sem.at[s, i * 4 + j],
-            device_id=(0, k // 4, k % 4),
+            device_id=(0, k // 2, 2 * (k % 2) + j // 2),
             device_id_type=MESH,
         )
 
@@ -129,17 +130,24 @@
             device_id_type=MESH,
         )
 
+    for k in range(4):
+        @pl.when(me != init_target(k))
+        def _():
+            init_copy(k).start()
+
+        @pl.when(me == init_target(k))
+        def _():
+            pltpu.make_async_copy(
+                hin_ref.at[k // 2], hid.at[s, i * 4 + j], hid_sem.at[s, i * 4 + j]
+            ).start()
+
     for k in range(8):
         @pl.when(me != k)
         def _():
-            init_copy(k).start()
             first_copy(k).start()
 
         @pl.when(me == k)
         def _():
-            pltpu.make_async_copy(
-                hin_ref.at[k // 4], hid.at[s, i * 4 + j], hid_sem.at[s, i * 4 + j]
-            ).start()
             pltpu.make_async_copy(
                 stat_first.at[1 - k // 4], stat_in.at[s, i * 4 + j], stat_rsem.at[s, i * 4 + j]
             ).start()
@@ -200,23 +208,23 @@
         def take(ref, sem):
             pltpu.make_async_copy(ref, ref, sem).wait()
 
+        for e in range(2):
+            for side in range(2):
+                g = 2 * (2 * side + parity) + e
+                take(hid.at[m, g], hid_sem.at[m, g])
+                forward_copy(m, e, side).start()
+        for e in range(2):
+            for side in range(2):
+                g = 2 * (2 * side + 1 - parity) + e
+                take(hid.at[m, g], hid_sem.at[m, g])
+
         @pl.when(s == 0)
         def _():
             for r in range(8):
-                take(hid.at[m, r], hid_sem.at[m, r])
                 take(stat_in.at[m, r], stat_rsem.at[m, r])
 
         @pl.when(s > 0)
         def _():
-            for e in range(2):
-                for side in range(2):
-                    g = 2 * (2 * side + parity) + e
-                    take(hid.at[m, g], hid_sem.at[m, g])
-                    forward_copy(m, e, side).start()
-            for e in range(2):
-                for side in range(2):
-                    g = 2 * (2 * side + 1 - parity) + e
-                    take(hid.at[m, g], hid_sem.at[m, g])
             for r in range(4):
                 take(stat_in.at[m, pl.ds(2 * r, 2)], stat_rsem.at[m, r])
 
@@ -294,7 +302,7 @@
             cols = slice(h * head_dim, (h + 1) * head_dim)
             values = kv[1, :, :, cols].reshape(sections * micro, head_dim)
             mixed = jnp.dot(weights, values, preferred_element_type=jnp.float32)
-            outs.append((mixed / total).astype(jnp.bfloat16))
+            outs.append((mixed * (1.0 / total)).astype(jnp.bfloat16))
         attended = jnp.concatenate(outs, axis=1)
         y = slab(jnp.dot(attended, wo[sel], preferred_element_type=jnp.float32))
         y_own[...] = y
@@ -348,10 +356,14 @@
 
         stage_d(m, sel)
 
+    for k in range(4):
+        @pl.when(me != init_target(k))
+        def _():
+            init_copy(k).wait_send()
+
     for k in range(8):
         @pl.when(me != k)
         def _():
-            init_copy(k).wait_send()
             first_copy(k).wait_send()
 
     @pl.loop(0, sections)
@@ -362,11 +374,9 @@
             for o in (1, 2, 3):
                 y_copy(m, o, e).wait_send()
 
-        @pl.when(s > 0)
-        def _():
-            for e in range(2):
-                for side in range(2):
-                    forward_copy(m, e, side).wait_send()
+        for e in range(2):
+            for side in range(2):
+                forward_copy(m, e, side).wait_send()
 
         @pl.when(s < last)
         def _():
@@ -406,7 +416,7 @@
     quarter = half // 2
     hin = hidden_in[0].reshape(rows, 2, 2, quarter)
     hin = jnp.transpose(hin, (1, 2, 0, 3)).reshape(2, 2 * rows, quarter)
-    pieces = -(-3 * local_width // 256)
+    pieces = 3
     bf16, f32 = jnp.bfloat16, jnp.float32
     dma = pltpu.SemaphoreType.DMA
     vmem = pl.BlockSpec(memory_space=pltpu.VMEM)
@@ -434,7 +444,7 @@
             pltpu.VMEM((2, half, 3 * local_width), bf16),
             pltpu.VMEM((2, local_width, half), bf16),
             pltpu.VMEM((2, sections, micro, local_width), bf16),
-            dma((8,)),
+            dma((4,)),
             dma((sections, 8)),
             dma((sections, 4)),
             dma((8,)),

time: 106 us -> 102 us (0.962)
  Pallas kernels: 104 us -> 99.5 us
    pallas_call x1, Pallas kernels: 104 us -> 99.5 us  [fused(): pl.pallas_call(functools.partial(pipe_kernel, sections, dual_count, heads...]
where the time goes in v3:
time: 102 us
  Pallas kernels  99.5 us (98%)
  local copies, waits for them, and re-layouts  1.42 us (1%)
    pallas_call x1, Pallas kernels, fused(): pl.pallas_call(functools.partial(pipe_kernel, sections, dual_count, heads...  99.5 us

profile of v3, /device:TPU:25, one launch (start us, length us, event | category | flops | bytes accessed | tf_op | source)
XLA Modules:
  0.0 101.6 jit_solution(8876046675350437572)
XLA Ops:
  0.7 99.5 %shard_map.91 = bf16[2,16,768]{2,1,0:T(8,128)(2,1)} custom-call(s32[1]{0:T(128)S(6)} %copy.11.len_ref, bf16[2,16,768]{2,1,0:T(8,128)(2,1)} %bitcast.26, f32[3,2,3072]{2,1,0:T(2,128)} %bitcast.25, f32[2,2,128]{2,1,0:T(2,128)} %bitcast.27, bf16[3,1536,384]{2,1,0:T(8,128)(2,1)} %bitcast.21, bf16[2,3,1536,384]{3,2,1,0:T(8,128)(2,1)} %bitcast.20, ...), custom_call_target="tpu_custom_call" | custom-call | flops 1207959552 | bytes 9437184 | tf_op jit(solution)/shard_map/pallas_call | solution.py:424
  100.2 1.4 %copy.12 = bf16[1,8,3072]{2,1,0:T(8,128)(2,1)} copy(bf16[1,8,3072]{2,1,0:T(8,128)(2,1)} %bitcast.24) | data formatting | bytes 98304
